TPU v7x, 256 devices: a whole 4x4x8 slice. The times are simulated.
256 devices in a mesh: section: 2 (over y_lo), fsdp: 32 (over x, z), dp: 4 (over y_hi, core).
Axes of the slice: x: 4, y: 4 (y_hi: 2, y_lo: 2; y = y_hi * 2 + y_lo), z: 8, core: 2. Of those that a mesh axis runs over, the one named last changes fastest.
Arguments:
- activations: bfloat16 [2, 4, 4096, 3584], P('section', None, ('fsdp', 'dp')), may hold values from -6 to 6
- out_grad: bfloat16 [2, 4, 4096, 14336], P('section', None, ('fsdp', 'dp')), may hold values from -6 to 6
- blocks: bfloat16 [2, 128, 128, 128], P('section', 'fsdp'), may hold values from -0.5 to 0.5
- pattern: int32 [2, 128, 2], P('section', 'fsdp'), may hold values from 0 to 111, as said below
- order: int32 [4], replicated, may hold values from 0 to 3, each once
Outputs:
- received: bfloat16 [2, 4, 4096, 3584], P('section', None, ('fsdp', 'dp'))
- weight_grad: float32 [2, 128, 128, 128], P('section', 'fsdp')
Inputs may be any that keep to these rules, and one draw needn't show every extreme that they name: pattern[s, b, 0] < 28 and pattern[s, b, 1] < 112; no two blocks of one section share both indices; within a section the blocks stand in ascending order of (row, column). `order`: a permutation of the microbatches.
All inputs are finite; a program needn't handle non-finite values.
Results may differ from a plain program's by a relative error of at most 0.0049.
Values may be sent and summed in bfloat16 or wider, within the bound.
A program may use at most 128 MiB of HBM per device.

v0:
```python
import math
import jax
import jax.numpy as jnp
from jax import lax
from jax.sharding import PartitionSpec as P


def passed_along(block, axis, distance):
    devices = range(lax.axis_size(axis))
    route = [(i - distance, i) for i in devices if i - distance in devices]
    return lax.ppermute(block, axis, route)


def silu_slope(pre_act):
    sigmoid_val = jax.nn.sigmoid(pre_act)
    return sigmoid_val * (1.0 + pre_act * (1.0 - sigmoid_val))


def in_groups(step_fn, running, shard_blocks):
    block_count = shard_blocks.shape[0]
    group_size = math.gcd(block_count, 32)

    def one_group(number, carried):
        segment = lax.dynamic_slice_in_dim(shard_blocks, number * group_size, group_size, 0)
        return step_fn(carried, segment, number * group_size)

    return lax.fori_loop(0, block_count // group_size, one_group, running)


def local(activations, out_grad, blocks, pattern, order):
    block_size = blocks.shape[-1]
    micro_count = activations.shape[1]
    tok_rows = activations.shape[1] * activations.shape[2]
    row_count = activations.shape[3] // block_size
    col_count = out_grad.shape[3] // block_size
    features = activations[0].reshape(tok_rows, row_count, block_size)
    hidden_grad = out_grad[0].reshape(tok_rows, out_grad.shape[3])
    own_blocks = blocks[0]
    all_indices = lax.all_gather(pattern[0], "fsdp", axis=0, tiled=True)

    def forward_step(running, shard_blocks, first_block):
        indices = lax.dynamic_slice_in_dim(all_indices, first_block, shard_blocks.shape[0], 0)
        rows_in = jnp.take(features, indices[:, 0], axis=1)
        product = jnp.einsum(
            "tbk,bkn->tbn", rows_in, shard_blocks, preferred_element_type=jnp.float32
        )
        return running.at[:, indices[:, 1]].add(product)

    pre_zero = jnp.zeros((tok_rows, col_count, block_size), jnp.float32)
    pre_act = in_groups(
        forward_step, pre_zero, lax.all_gather(own_blocks, "fsdp", axis=0, tiled=True)
    )
    act_grad = (hidden_grad.astype(jnp.float32) * silu_slope(pre_act.reshape(tok_rows, -1))).astype(
        jnp.bfloat16
    )
    grad_cols = act_grad.reshape(tok_rows, col_count, block_size)

    def backward_step(running, shard_blocks, first_block):
        indices = lax.dynamic_slice_in_dim(all_indices, first_block, shard_blocks.shape[0], 0)
        cols_in = jnp.take(grad_cols, indices[:, 1], axis=1)
        product = jnp.einsum(
            "tbn,bkn->tbk", cols_in, shard_blocks, preferred_element_type=jnp.float32
        )
        return running.at[:, indices[:, 0]].add(product)

    back_zero = jnp.zeros((tok_rows, row_count, block_size), jnp.float32)
    input_grad = in_groups(
        backward_step, back_zero, lax.all_gather(own_blocks, "fsdp", axis=0, tiled=True)
    )
    input_grad = input_grad.astype(jnp.bfloat16).reshape(
        micro_count, activations.shape[2], activations.shape[3]
    )
    ordered = jnp.take(input_grad, order, axis=0)
    received = passed_along(ordered, "section", -1)
    indices = all_indices
    rows_in = jnp.take(features, indices[:, 0], axis=1)
    cols_in = jnp.take(grad_cols, indices[:, 1], axis=1)
    owned_grads = lax.psum_scatter(
        jnp.einsum("tbk,tbn->bkn", rows_in, cols_in, preferred_element_type=jnp.float32),
        "fsdp",
        scatter_dimension=0,
        tiled=True,
    )
    summed = lax.psum(owned_grads, "dp")
    grad_scale = 1.0 / math.sqrt(tok_rows * lax.axis_size("fsdp") * lax.axis_size("dp"))
    return (received[None], (summed * grad_scale)[None])


def solution(mesh):
    in_specs = (
        P("section", None, ("fsdp", "dp"), None),
        P("section", None, ("fsdp", "dp"), None),
        P("section", "fsdp", None, None),
        P("section", "fsdp", None),
        P(),
    )
    out_specs = (P("section", None, ("fsdp", "dp"), None), P("section", "fsdp", None, None))
    return jax.shard_map(local, mesh=mesh, in_specs=in_specs, out_specs=out_specs, check_vma=False)
```

profile of v0, /device:TPU:1, one launch (start us, length us, event | category | flops | bytes accessed | tf_op | source)
XLA Modules:
  0.0 444.8 jit_solution(14893785248069533942)
XLA Ops:
  8.7 40.7 %all-gather = s32[1,128,2]{2,0,1:T(1,128)S(1)} all-gather(s32[1,4,2]{2,0,1:T(1,128)S(1)} %copy.31), channel_id=2, replica_groups=mesh['section'=2,'fsdp'=32,'dp'=4] {'fsdp'}, dimensions={1}, use_global_device_ids=true | all-gather | bytes 1056 | tf_op jit(solution)/shard_map/all_gather | solution.py:39
  51.5 5.9 %copy.41 = f32[16,8,112,128]{3,2,1,0:T(8,128)} copy(bf16[16,8,112,128]{3,1,2,0:T(8,128)(2,1)} %bitcast.51) | data formatting | bytes 11010048
  57.5 3.1 gather_fusion.3
  60.8 32.7 %all-gather.4.cloned.1.call-done = bf16[1,128,128,128]{3,2,0,1:T(8,128)(2,1)} async-done(((bf16[1,4,128,128]{3,2,0,1:T(8,128)(2,1)}), bf16[1,128,128,128]{3,2,0,1:T(8,128)(2,1)}) %all-gather.4.cloned.1.call-update) | async-done | bytes 4194320 | tf_op jit(solution)/shard_map/all_gather | solution.py:68
  93.5 3.9 broadcast_in_dim.90
  97.5 40.1 %while.26 = (s32[]{:T(128)}, f32[128,112,128]{2,0,1:T(8,128)}, s32[128,2]{0,1:T(2,128)S(1)}, bf16[128,128,128]{2,1,0:T(8,128)(2,1)}, bf16[128,28,128]{2,0,1:T(8,...) while((s32[]{:T(128)}, f32[128,112,128]{2,0,1:T(8,128)}, s32[128,2]{0,1:T(2,128)S(1)}, ...), condition=%wide.region_2.3_spmd, body=%wide.region_0.2_spmd.sunk | while | flops 135267712 | bytes 12588755 | solution.py:27
  101.3 6.2 %scatter_fusion = f32[128,112,128]{2,0,1:T(8,128)} fusion(f32[128,112,128]{2,0,1:T(8,128)} %get-tuple-element.332, s32[32]{0:T(128)S(1)} %get-tuple-element.313, f32[32,128,128]{2,1,0:T(8,128)S(1)} %fusion.43), kind=kCustom, calls=%fused_computation.5.clone.1 | custom fusion | flops 524288 | bytes 6291584 | tf_op jit(solution)/shard_map/while/body/eval_jaxpr/scatter-add | solution.py:47
  111.3 6.2 %scatter_fusion = f32[128,112,128]{2,0,1:T(8,128)} fusion(f32[128,112,128]{2,0,1:T(8,128)} %get-tuple-element.332, s32[32]{0:T(128)S(1)} %get-tuple-element.313, f32[32,128,128]{2,1,0:T(8,128)S(1)} %fusion.43), kind=kCustom, calls=%fused_computation.5.clone.1 | custom fusion | flops 524288 | bytes 6291584 | tf_op jit(solution)/shard_map/while/body/eval_jaxpr/scatter-add | solution.py:47
  121.3 6.2 %scatter_fusion = f32[128,112,128]{2,0,1:T(8,128)} fusion(f32[128,112,128]{2,0,1:T(8,128)} %get-tuple-element.332, s32[32]{0:T(128)S(1)} %get-tuple-element.313, f32[32,128,128]{2,1,0:T(8,128)S(1)} %fusion.43), kind=kCustom, calls=%fused_computation.5.clone.1 | custom fusion | flops 524288 | bytes 6291584 | tf_op jit(solution)/shard_map/while/body/eval_jaxpr/scatter-add | solution.py:47
  131.3 6.2 %scatter_fusion = f32[128,112,128]{2,0,1:T(8,128)} fusion(f32[128,112,128]{2,0,1:T(8,128)} %get-tuple-element.332, s32[32]{0:T(128)S(1)} %get-tuple-element.313, f32[32,128,128]{2,1,0:T(8,128)S(1)} %fusion.43), kind=kCustom, calls=%fused_computation.5.clone.1 | custom fusion | flops 524288 | bytes 6291584 | tf_op jit(solution)/shard_map/while/body/eval_jaxpr/scatter-add | solution.py:47
  137.5 8.5 %fusion.20 = bf16[128,112,128]{2,0,1:T(8,128)(2,1)} fusion(f32[128,112,128]{2,1,0:T(8,128)} %bitcast.49, f32[128,112,128]{2,0,1:T(8,128)} %get-tuple-element.190), kind=kLoop, calls=%fused_computation.38 | loop fusion | flops 16515072 | bytes 18350080 | tf_op jit(solution)/shard_map/convert_element_type | solution.py:53
  146.0 5.1 %gather_fusion.4 = bf16[128,128,128]{2,1,0:T(8,128)(2,1)} fusion(bf16[128,112,128]{2,0,1:T(8,128)(2,1)} %fusion.20, s32[1024]{0:T(1024)S(1)} %get-tuple-element.250), kind=kCustom, calls=%fused_computation.4 | custom fusion | bytes 8389120 | tf_op jit(solution)/shard_map/jit(_take)/gather | solution.py:77
  151.1 8.5 %fusion.21 = f32[128,128,128]{2,1,0:T(8,128)} fusion(bf16[128,128,128]{2,1,0:T(8,128)(2,1)} %gather_fusion.4, bf16[128,128,128]{2,1,0:T(8,128)(2,1)} %gather_fusion.3, pred[128]{0:T(512)(128)(4,1)S(1)} %get-tuple-element.223, pred[128]{0:T(512)(128)(4,1)S(1)} %get-tuple-element.222), kind=kOutput, calls=%fused_computation.39 | convolution fusion | flops 541065216 | bytes 16777472 | tf_op jit(solution)/shard_map/tbk,tbn->bkn/dot_general | solution.py:79
  161.8 45.7 %while.27 = (s32[]{:T(128)}, f32[128,28,128]{2,0,1:T(8,128)}, s32[128,2]{0,1:T(2,128)S(1)}, bf16[128,128,128]{2,1,0:T(8,128)(2,1)}, bf16[128,112,128]{2,0,1:T(8,...) while((s32[]{:T(128)}, f32[128,28,128]{2,0,1:T(8,128)}, s32[128,2]{0,1:T(2,128)S(1)}, ...), condition=%wide.region_5.6_spmd, body=%wide.region_3.5_spmd.sunk | while | flops 135267712 | bytes 12588755 | solution.py:27
  161.9 2.8 gather_fusion.1
  166.8 6.4 %scatter_fusion.1 = f32[128,28,128]{2,0,1:T(8,128)} fusion(f32[128,28,128]{2,0,1:T(8,128)} %get-tuple-element.359, s32[32]{0:T(128)S(1)} %get-tuple-element.320, f32[32,128,128]{2,1,0:T(8,128)S(1)} %fusion.47), kind=kCustom, calls=%fused_computation.6.clone.1 | custom fusion | flops 524288 | bytes 6291584 | tf_op jit(solution)/shard_map/while/body/eval_jaxpr/scatter-add | solution.py:64
  173.3 2.8 gather_fusion.1
  178.3 6.5 %scatter_fusion.1 = f32[128,28,128]{2,0,1:T(8,128)} fusion(f32[128,28,128]{2,0,1:T(8,128)} %get-tuple-element.359, s32[32]{0:T(128)S(1)} %get-tuple-element.320, f32[32,128,128]{2,1,0:T(8,128)S(1)} %fusion.47), kind=kCustom, calls=%fused_computation.6.clone.1 | custom fusion | flops 524288 | bytes 6291584 | tf_op jit(solution)/shard_map/while/body/eval_jaxpr/scatter-add | solution.py:64
  184.8 2.8 gather_fusion.1
  189.8 6.3 %scatter_fusion.1 = f32[128,28,128]{2,0,1:T(8,128)} fusion(f32[128,28,128]{2,0,1:T(8,128)} %get-tuple-element.359, s32[32]{0:T(128)S(1)} %get-tuple-element.320, f32[32,128,128]{2,1,0:T(8,128)S(1)} %fusion.47), kind=kCustom, calls=%fused_computation.6.clone.1 | custom fusion | flops 524288 | bytes 6291584 | tf_op jit(solution)/shard_map/while/body/eval_jaxpr/scatter-add | solution.py:64
  196.1 2.9 gather_fusion.1
  201.2 6.3 %scatter_fusion.1 = f32[128,28,128]{2,0,1:T(8,128)} fusion(f32[128,28,128]{2,0,1:T(8,128)} %get-tuple-element.359, s32[32]{0:T(128)S(1)} %get-tuple-element.320, f32[32,128,128]{2,1,0:T(8,128)S(1)} %fusion.47), kind=kCustom, calls=%fused_computation.6.clone.1 | custom fusion | flops 524288 | bytes 6291584 | tf_op jit(solution)/shard_map/while/body/eval_jaxpr/scatter-add | solution.py:64
  212.3 172.1 %reduce-scatter.2.cloned.1.call-done = f32[4,128,128]{2,1,0:T(8,128)} async-done(((f32[128,128,128]{2,1,0:T(8,128)}), f32[4,128,128]{2,1,0:T(8,128)}) %reduce-scatter.2.cloned.1.call-update) | async-done | bytes 262160 | tf_op jit(solution)/shard_map/reduce_scatter | solution.py:78
  384.5 51.2 %all-reduce.2.cloned.1.call-done = f32[4,128,128]{2,1,0:T(8,128)} async-done(((f32[4,128,128]{2,1,0:T(8,128)}), f32[4,128,128]{2,1,0:T(8,128)}) %all-reduce.2.cloned.1.call-update) | async-done | bytes 262160 | tf_op jit(solution)/shard_map/psum | solution.py:84
  (72 shorter events, 37.5 us)
Async XLA Ops:
  7.2 86.3 %all-gather.4.cloned.1.call-start = ((), (), s32[]{:S(2)}) async-start(), calls=%async_computation.3 | async-start | bytes 4325376 | tf_op jit(solution)/shard_map/all_gather | solution.py:68
  7.9 376.5 %reduce-scatter.2.cloned.1.call-start = ((), (), s32[]{:S(2)}) async-start(), calls=%async_computation.1 | async-start | bytes 8650752 | tf_op jit(solution)/shard_map/reduce_scatter | solution.py:78
  159.6 0.7 copy-start
  159.7 276.0 %all-reduce.2.cloned.1.call-start = ((), (), s32[]{:S(2)}) async-start(), calls=%async_computation.2 | async-start | bytes 524288 | tf_op jit(solution)/shard_map/psum | solution.py:84
  211.0 173.4 %collective-permute-start = (bf16[4,32,3584]{2,1,0:T(8,128)(2,1)S(1)}, bf16[4,32,3584]{2,1,0:T(8,128)(2,1)S(1)}, u32[]{:S(2)}, u32[]{:S(2)}) collective-permute-start(bf16[4,32,3584]{2,1,0:T(8,128)(2,1)S(1)} %broadcast_select_fusion), channel_id=1, source_target_pairs={{128,0},{129,1},{130,2},{131,3},{132,4},{133,5},{134,6},{135,7},{1... | collective-permute-start | bytes 2752520 | tf_op jit(solution)/shard_map/ppermute | solution.py:11
Sparse Core Ops, SparseCore 0:
  10.6 82.8 all-gather.3
  159.8 224.6 reduce-scatter.1
  387.3 48.3 all-reduce.1
where the time goes:
time: 447 us; the launch traced here: 445 us
  waiting for transfers between devices  257 us (57%)
  other arithmetic  62.9 us (14%)
  local copies, waits for them, and re-layouts  43.9 us (10%)
  blocking collectives  40.7 us (9%)
  matrix products  25.1 us (6%)
  between operations  13.8 us (3%)
    reduce_scatter x1, waiting for transfers between devices, local(): lax.psum_scatter(jnp.einsum('tbk,tbn->bkn', rows_in, cols_in, preferred_e...  172 us
    psum x1, waiting for transfers between devices, local(): summed = lax.psum(owned_grads, 'dp')  51.2 us
    all_gather x1, blocking collectives, local(): all_indices = lax.all_gather(pattern[0], 'fsdp', axis=0, tiled=True)  40.7 us
    all_gather x1, waiting for transfers between devices, local(): lax.all_gather(own_blocks, 'fsdp', axis=0, tiled=True)  32.7 us
    scatter-add x4, other arithmetic, backward_step(): return running.at[:, indices[:, 0]].add(product)  25.5 us
    scatter-add x4, other arithmetic, forward_step(): return running.at[:, indices[:, 1]].add(product)  24.8 us
    gather x4, local copies, waits for them, and re-layouts, backward_step(): cols_in = jnp.take(grad_cols, indices[:, 1], axis=1)  11.3 us
  transfers between devices with their start and end apart: 4, of which 3 were waited for; matrix products, arithmetic and copies ran while one was open for 14% of the time, Pallas kernels for 0%

commit v1 on v0

--- a/solution.py
+++ b/solution.py
@@ -81,7 +81,7 @@
         scatter_dimension=0,
         tiled=True,
     )
-    summed = lax.psum(owned_grads, "dp")
+    summed = jnp.sum(lax.all_gather(owned_grads, "dp"), axis=0)
     grad_scale = 1.0 / math.sqrt(tok_rows * lax.axis_size("fsdp") * lax.axis_size("dp"))
     return (received[None], (summed * grad_scale)[None])
 

time: 447 us -> 425 us (0.951)
  waiting for transfers between devices: 257 us -> 233 us
    psum x1 -> x0, waiting for transfers between devices: 51.2 us -> none  [local(): summed = lax.psum(owned_grads, 'dp')]
    ppermute x1, waiting for transfers between devices: 0.01 us -> 17.8 us  [passed_along(): return lax.ppermute(block, axis, route)]
    all_gather x0 -> x1, waiting for transfers between devices: none -> 8.71 us  [local(): summed = jnp.sum(lax.all_gather(owned_grads, 'dp'), axis=0)]
  transfers between devices with their start and end apart: 4 -> 4, of which waited for: 3 -> 4; matrix products, arithmetic and copies ran while one was open for 14% -> 15% of each run, Pallas kernels for 0% -> 0%
where the time goes in v1:
time: 425 us; the launch traced here: 422 us
  waiting for transfers between devices  233 us (55%)
  other arithmetic  63.2 us (15%)
  local copies, waits for them, and re-layouts  43.9 us (10%)
  blocking collectives  40.7 us (10%)
  matrix products  25.1 us (6%)
  between operations  13.8 us (3%)
    reduce_scatter x1, waiting for transfers between devices, local(): lax.psum_scatter(jnp.einsum('tbk,tbn->bkn', rows_in, cols_in, preferred_e...  174 us
    all_gather x1, blocking collectives, local(): all_indices = lax.all_gather(pattern[0], 'fsdp', axis=0, tiled=True)  40.7 us
    all_gather x1, waiting for transfers between devices, local(): lax.all_gather(own_blocks, 'fsdp', axis=0, tiled=True)  32.7 us
    scatter-add x4, other arithmetic, backward_step(): return running.at[:, indices[:, 0]].add(product)  25.5 us
    scatter-add x4, other arithmetic, forward_step(): return running.at[:, indices[:, 1]].add(product)  24.8 us
    ppermute x1, waiting for transfers between devices, passed_along(): return lax.ppermute(block, axis, route)  17.8 us
    gather x4, local copies, waits for them, and re-layouts, backward_step(): cols_in = jnp.take(grad_cols, indices[:, 1], axis=1)  11.3 us
    all_gather x1, waiting for transfers between devices, local(): summed = jnp.sum(lax.all_gather(owned_grads, 'dp'), axis=0)  8.71 us
  transfers between devices with their start and end apart: 4, of which 4 were waited for; matrix products, arithmetic and copies ran while one was open for 15% of the time, Pallas kernels for 0%

profile of v1, /device:TPU:1, one launch (start us, length us, event | category | flops | bytes accessed | tf_op | source)
XLA Modules:
  0.0 421.9 jit_solution(7748221262667150776)
XLA Ops:
  8.7 40.7 %all-gather = s32[1,128,2]{2,0,1:T(1,128)S(1)} all-gather(s32[1,4,2]{2,0,1:T(1,128)S(1)} %copy.31), channel_id=2, replica_groups=mesh['section'=2,'fsdp'=32,'dp'=4] {'fsdp'}, dimensions={1}, use_global_device_ids=true | all-gather | bytes 1056 | tf_op jit(solution)/shard_map/all_gather | solution.py:39
  51.5 5.9 %copy.41 = f32[16,8,112,128]{3,2,1,0:T(8,128)} copy(bf16[16,8,112,128]{3,1,2,0:T(8,128)(2,1)} %bitcast.52) | data formatting | bytes 11010048
  57.5 3.1 gather_fusion.3
  60.8 32.7 %all-gather.6.cloned.1.call-done = bf16[1,128,128,128]{3,2,0,1:T(8,128)(2,1)} async-done(((bf16[1,4,128,128]{3,2,0,1:T(8,128)(2,1)}), bf16[1,128,128,128]{3,2,0,1:T(8,128)(2,1)}) %all-gather.6.cloned.1.call-update) | async-done | bytes 4194320 | tf_op jit(solution)/shard_map/all_gather | solution.py:68
  93.5 3.9 broadcast_in_dim.88
  97.5 40.1 %while.26 = (s32[]{:T(128)}, f32[128,112,128]{2,0,1:T(8,128)}, s32[128,2]{0,1:T(2,128)S(1)}, bf16[128,128,128]{2,1,0:T(8,128)(2,1)}, bf16[128,28,128]{2,0,1:T(8,...) while((s32[]{:T(128)}, f32[128,112,128]{2,0,1:T(8,128)}, s32[128,2]{0,1:T(2,128)S(1)}, ...), condition=%wide.region_2.3_spmd, body=%wide.region_0.2_spmd.sunk | while | flops 135267712 | bytes 12588755 | solution.py:27
  101.3 6.2 %scatter_fusion = f32[128,112,128]{2,0,1:T(8,128)} fusion(f32[128,112,128]{2,0,1:T(8,128)} %get-tuple-element.332, s32[32]{0:T(128)S(1)} %get-tuple-element.313, f32[32,128,128]{2,1,0:T(8,128)S(1)} %fusion.43), kind=kCustom, calls=%fused_computation.5.clone.1 | custom fusion | flops 524288 | bytes 6291584 | tf_op jit(solution)/shard_map/while/body/eval_jaxpr/scatter-add | solution.py:47
  111.3 6.2 %scatter_fusion = f32[128,112,128]{2,0,1:T(8,128)} fusion(f32[128,112,128]{2,0,1:T(8,128)} %get-tuple-element.332, s32[32]{0:T(128)S(1)} %get-tuple-element.313, f32[32,128,128]{2,1,0:T(8,128)S(1)} %fusion.43), kind=kCustom, calls=%fused_computation.5.clone.1 | custom fusion | flops 524288 | bytes 6291584 | tf_op jit(solution)/shard_map/while/body/eval_jaxpr/scatter-add | solution.py:47
  121.3 6.2 %scatter_fusion = f32[128,112,128]{2,0,1:T(8,128)} fusion(f32[128,112,128]{2,0,1:T(8,128)} %get-tuple-element.332, s32[32]{0:T(128)S(1)} %get-tuple-element.313, f32[32,128,128]{2,1,0:T(8,128)S(1)} %fusion.43), kind=kCustom, calls=%fused_computation.5.clone.1 | custom fusion | flops 524288 | bytes 6291584 | tf_op jit(solution)/shard_map/while/body/eval_jaxpr/scatter-add | solution.py:47
  131.3 6.2 %scatter_fusion = f32[128,112,128]{2,0,1:T(8,128)} fusion(f32[128,112,128]{2,0,1:T(8,128)} %get-tuple-element.332, s32[32]{0:T(128)S(1)} %get-tuple-element.313, f32[32,128,128]{2,1,0:T(8,128)S(1)} %fusion.43), kind=kCustom, calls=%fused_computation.5.clone.1 | custom fusion | flops 524288 | bytes 6291584 | tf_op jit(solution)/shard_map/while/body/eval_jaxpr/scatter-add | solution.py:47
  137.5 8.5 %fusion.20 = bf16[128,112,128]{2,0,1:T(8,128)(2,1)} fusion(f32[128,112,128]{2,1,0:T(8,128)} %bitcast.50, f32[128,112,128]{2,0,1:T(8,128)} %get-tuple-element.190), kind=kLoop, calls=%fused_computation.38 | loop fusion | flops 16515072 | bytes 18350080 | tf_op jit(solution)/shard_map/convert_element_type | solution.py:53
  146.0 5.1 %gather_fusion.4 = bf16[128,128,128]{2,1,0:T(8,128)(2,1)} fusion(bf16[128,112,128]{2,0,1:T(8,128)(2,1)} %fusion.20, s32[1024]{0:T(1024)S(1)} %get-tuple-element.250), kind=kCustom, calls=%fused_computation.4 | custom fusion | bytes 8389120 | tf_op jit(solution)/shard_map/jit(_take)/gather | solution.py:77
  151.1 8.5 %fusion.21 = f32[128,128,128]{2,1,0:T(8,128)} fusion(bf16[128,128,128]{2,1,0:T(8,128)(2,1)} %gather_fusion.4, bf16[128,128,128]{2,1,0:T(8,128)(2,1)} %gather_fusion.3, pred[128]{0:T(512)(128)(4,1)S(1)} %get-tuple-element.223, pred[128]{0:T(512)(128)(4,1)S(1)} %get-tuple-element.222), kind=kOutput, calls=%fused_computation.39 | convolution fusion | flops 541065216 | bytes 16777472 | tf_op jit(solution)/shard_map/tbk,tbn->bkn/dot_general | solution.py:79
  161.8 45.7 %while.27 = (s32[]{:T(128)}, f32[128,28,128]{2,0,1:T(8,128)}, s32[128,2]{0,1:T(2,128)S(1)}, bf16[128,128,128]{2,1,0:T(8,128)(2,1)}, bf16[128,112,128]{2,0,1:T(8,...) while((s32[]{:T(128)}, f32[128,28,128]{2,0,1:T(8,128)}, s32[128,2]{0,1:T(2,128)S(1)}, ...), condition=%wide.region_5.6_spmd, body=%wide.region_3.5_spmd.sunk | while | flops 135267712 | bytes 12588755 | solution.py:27
  161.9 2.8 gather_fusion.1
  166.8 6.4 %scatter_fusion.1 = f32[128,28,128]{2,0,1:T(8,128)} fusion(f32[128,28,128]{2,0,1:T(8,128)} %get-tuple-element.359, s32[32]{0:T(128)S(1)} %get-tuple-element.320, f32[32,128,128]{2,1,0:T(8,128)S(1)} %fusion.47), kind=kCustom, calls=%fused_computation.6.clone.1 | custom fusion | flops 524288 | bytes 6291584 | tf_op jit(solution)/shard_map/while/body/eval_jaxpr/scatter-add | solution.py:64
  178.3 6.5 %scatter_fusion.1 = f32[128,28,128]{2,0,1:T(8,128)} fusion(f32[128,28,128]{2,0,1:T(8,128)} %get-tuple-element.359, s32[32]{0:T(128)S(1)} %get-tuple-element.320, f32[32,128,128]{2,1,0:T(8,128)S(1)} %fusion.47), kind=kCustom, calls=%fused_computation.6.clone.1 | custom fusion | flops 524288 | bytes 6291584 | tf_op jit(solution)/shard_map/while/body/eval_jaxpr/scatter-add | solution.py:64
  184.8 2.8 gather_fusion.1
  189.8 6.3 %scatter_fusion.1 = f32[128,28,128]{2,0,1:T(8,128)} fusion(f32[128,28,128]{2,0,1:T(8,128)} %get-tuple-element.359, s32[32]{0:T(128)S(1)} %get-tuple-element.320, f32[32,128,128]{2,1,0:T(8,128)S(1)} %fusion.47), kind=kCustom, calls=%fused_computation.6.clone.1 | custom fusion | flops 524288 | bytes 6291584 | tf_op jit(solution)/shard_map/while/body/eval_jaxpr/scatter-add | solution.py:64
  196.1 2.9 gather_fusion.1
  201.2 6.3 %scatter_fusion.1 = f32[128,28,128]{2,0,1:T(8,128)} fusion(f32[128,28,128]{2,0,1:T(8,128)} %get-tuple-element.359, s32[32]{0:T(128)S(1)} %get-tuple-element.320, f32[32,128,128]{2,1,0:T(8,128)S(1)} %fusion.47), kind=kCustom, calls=%fused_computation.6.clone.1 | custom fusion | flops 524288 | bytes 6291584 | tf_op jit(solution)/shard_map/while/body/eval_jaxpr/scatter-add | solution.py:64
  210.9 173.5 %reduce-scatter.2.cloned.1.call-done = f32[4,128,128]{2,1,0:T(8,128)} async-done(((f32[128,128,128]{2,1,0:T(8,128)}), f32[4,128,128]{2,1,0:T(8,128)}) %reduce-scatter.2.cloned.1.call-update) | async-done | bytes 262160 | tf_op jit(solution)/shard_map/reduce_scatter | solution.py:78
  385.9 17.8 %collective-permute-done = bf16[4,32,3584]{2,1,0:T(8,128)(2,1)S(1)} collective-permute-done((bf16[4,32,3584]{2,1,0:T(8,128)(2,1)S(1)}, bf16[4,32,3584]{2,1,0:T(8,128)(2,1)S(1)}, u32[]{:S(2)}, u32[]{:S(2)}) %collective-permute-start) | collective-permute-done | bytes 917536 | tf_op jit(solution)/shard_map/ppermute | solution.py:11
  403.7 8.7 %all-gather.8.cloned.1.call-done = f32[16,128,128]{2,1,0:T(8,128)} async-done(((f32[4,128,128]{2,1,0:T(8,128)}), f32[16,128,128]{2,1,0:T(8,128)}) %all-gather.8.cloned.1.call-update) | async-done | bytes 1048592 | tf_op jit(solution)/shard_map/all_gather | solution.py:84
  (73 shorter events, 40.7 us)
Async XLA Ops:
  7.2 86.3 %all-gather.6.cloned.1.call-start = ((), (), s32[]{:S(2)}) async-start(), calls=%async_computation.2 | async-start | bytes 4325376 | tf_op jit(solution)/shard_map/all_gather | solution.py:68
  7.9 376.5 %reduce-scatter.2.cloned.1.call-start = ((), (), s32[]{:S(2)}) async-start(), calls=%async_computation.1 | async-start | bytes 8650752 | tf_op jit(solution)/shard_map/reduce_scatter | solution.py:78
  159.6 0.7 copy-start
  159.7 252.8 %all-gather.8.cloned.1.call-start = ((), (), s32[]{:S(2)}) async-start(), calls=%async_computation.3 | async-start | bytes 1310720 | tf_op jit(solution)/shard_map/all_gather | solution.py:84
  384.6 19.1 %collective-permute-start = (bf16[4,32,3584]{2,1,0:T(8,128)(2,1)S(1)}, bf16[4,32,3584]{2,1,0:T(8,128)(2,1)S(1)}, u32[]{:S(2)}, u32[]{:S(2)}) collective-permute-start(bf16[4,32,3584]{2,1,0:T(8,128)(2,1)S(1)} %broadcast_select_fusion), channel_id=1, source_target_pairs={{128,0},{129,1},{130,2},{131,3},{132,4},{133,5},{134,6},{135,7},{1... | collective-permute-start | bytes 2752520 | tf_op jit(solution)/shard_map/ppermute | solution.py:11
Sparse Core Ops, SparseCore 0:
  10.6 82.8 all-gather.5
  159.8 224.5 reduce-scatter.1
  386.4 26.0 all-gather.7
